TPU v7x, 32 devices: a whole 2x2x4 slice. The times are simulated.
32 devices in a mesh: dp: 4 (over x, core), cell: 8 (over z, y).
Axes of the slice: x: 2, y: 2, z: 4, core: 2. Of those that a mesh axis runs over, the one named last changes fastest.
Arguments:
- probes: float32 [8, 32, 32, 128], P('cell', None, None, 'dp'), may hold values from -6 to 6
- diag_coef: float32 [8, 32, 32], P('cell'), may hold values from 1.5 to 3
- coupling: float32 [8, 32, 32], P('cell'), may hold values from 0.1 to 0.4
- jacobian: bfloat16 [16384, 8192], P('dp', 'cell'), may hold values from -0.0625 to 0.0625
- group_ids: int32 [16384], P('dp'), may hold values from 0 to 7
- group_weights: float32 [8], replicated, may hold values from 0.25 to 4
Outputs:
- action: float32 [8, 32, 32, 128], P('cell', None, None, 'dp')
All inputs are finite; a program needn't handle non-finite values.
Results may differ from a plain program's by a relative error of at most 0.0036.
Values may be sent and summed in bfloat16 or wider, within the bound.
A program may use at most 64 MiB of HBM per device.

v0:
```python
import jax
import jax.numpy as jnp
from jax import lax
from jax.sharding import PartitionSpec as P


def padded_2(cells, sides, width):
    for axis, dim in sides:
        count = lax.axis_size(axis)
        ends = count - 1
        head = lax.slice_in_dim(cells, 0, width, axis=dim)
        tail = lax.slice_in_dim(cells, cells.shape[dim] - width, cells.shape[dim], axis=dim)
        cells = jnp.concatenate(
            [
                lax.ppermute(tail, axis, [(i, (i + 1) % count) for i in range(ends)]),
                cells,
                lax.ppermute(head, axis, [((i + 1) % count, i) for i in range(ends)]),
            ],
            axis=dim,
        )
    return cells


def slab_sum(padded):
    inner = padded[1:-1]
    total = padded[2:] + padded[:-2]
    framed = jnp.pad(inner, ((0, 0), (1, 1), (1, 1), (0, 0)))
    total = total + framed[:, 2:, 1:-1] + framed[:, :-2, 1:-1]
    return total + framed[:, 1:-1, 2:] + framed[:, 1:-1, :-2]


def row_weights(group_ids, group_weights):
    labels = jnp.arange(group_weights.shape[0], dtype=jnp.int32)
    match = group_ids[:, None] == labels[None, :]
    return jnp.sum(jnp.where(match, group_weights[None, :], 0.0), axis=1)


def shards(probes, diag_coef, coupling, jacobian, group_ids, group_weights):
    depth, height, width, share = probes.shape
    diag_full = diag_coef[..., None]
    coup_full = coupling[..., None]
    ncells = depth * height * width
    padded = padded_2(coup_full * probes, (("cell", 0),), 1)
    prior = (diag_full * probes - slab_sum(padded)).astype(jnp.bfloat16).reshape(ncells, share)
    predicted = jnp.dot(
        jacobian,
        lax.all_gather(prior, "dp", axis=1, tiled=True),
        preferred_element_type=jnp.float32,
    )
    total = lax.psum(predicted, "cell")
    weighted = (row_weights(group_ids, group_weights)[:, None] * total).astype(jnp.bfloat16)
    back = lax.dot_general(
        jacobian, weighted, (((0,), (0,)), ((), ())), preferred_element_type=jnp.float32
    )
    mine = lax.psum_scatter(back, "dp", scatter_dimension=1, tiled=True).reshape(
        depth, height, width, share
    )
    padded_back = padded_2(mine, (("cell", 0),), 1)
    return probes + diag_full * mine - coup_full * slab_sum(padded_back)


def solution(mesh):
    return jax.shard_map(
        shards,
        mesh=mesh,
        in_specs=(
            P("cell", None, None, "dp"),
            P("cell", None, None),
            P("cell", None, None),
            P("dp", "cell"),
            P("dp"),
            P(),
        ),
        out_specs=P("cell", None, None, "dp"),
        check_vma=False,
    )
```

profile of v0, /device:TPU:0, one launch (start us, length us, event | category | flops | bytes accessed | tf_op | source)
XLA Modules:
  0.0 217.5 jit_solution(16011591104756948739)
XLA Ops:
  6.5 0.0 all-reduce.4.cloned.1.call-start
  6.5 0.0 copy-start.3
  6.5 0.0 copy-start.4
  6.5 1.3 broadcast_multiply_fusion
  7.8 1.3 collective-permute-start
  9.1 5.5 %collective-permute-start.1 = (f32[1,32,32,32]{3,2,1,0:T(8,128)S(1)}, f32[1,32,32,32]{3,2,1,0:T(8,128)S(1)}, u32[]{:S(2)}, u32[]{:S(2)}) collective-permute-start(f32[1,32,32,32]{3,2,1,0:T(8,128)S(1)} %broadcast_multiply_fusion), channel_id=1, source_target_pairs={{0,1},{1,2},{2,3},{3,4},{4,5},{5,6},{6,7},{8,9},{9,10},{10,11},{11... | collective-permute-start | bytes 393224 | tf_op jit(solution)/shard_map/ppermute | solution.py:15
  14.7 10.0 %collective-permute-done = f32[1,32,32,32]{3,2,1,0:T(8,128)S(1)} collective-permute-done((f32[1,32,32,32]{3,2,1,0:T(8,128)S(1)}, f32[1,32,32,32]{3,2,1,0:T(8,128)S(1)}, u32[]{:S(2)}, u32[]{:S(2)}) %collective-permute-start) | collective-permute-done | bytes 131104 | tf_op jit(solution)/shard_map/ppermute | solution.py:17
  24.6 11.4 %collective-permute-done.1 = f32[1,32,32,32]{3,2,1,0:T(8,128)S(1)} collective-permute-done((f32[1,32,32,32]{3,2,1,0:T(8,128)S(1)}, f32[1,32,32,32]{3,2,1,0:T(8,128)S(1)}, u32[]{:S(2)}, u32[]{:S(2)}) %collective-permute-start.1) | collective-permute-done | bytes 131104 | tf_op jit(solution)/shard_map/ppermute | solution.py:15
  36.0 1.3 fusion.6
  37.3 0.1 copy.21
  37.5 5.8 %all_gather.3 = bf16[1024,128]{0,1:T(8,128)(2,1)S(1)} all-gather(bf16[1024,32]{0,1:T(8,128)(2,1)S(1)} %copy.21), channel_id=1, replica_groups=mesh['dp'=4,'cell'=8] {'dp'}, dimensions={1}, use_global_device_ids=true | all-gather | bytes 327680 | tf_op jit(solution)/shard_map/all_gather | solution.py:47
  43.2 7.5 %convolution_bitcast_fusion = f32[4096,128]{0,1:T(8,128)} fusion(bf16[1024,128]{0,1:T(8,128)(2,1)S(1)} %all_gather.3, bf16[4096,1024]{1,0:T(8,128)(2,1)} %param.9), kind=kOutput, calls=%fused_computation | convolution fusion | flops 1073741824 | bytes 10747904 | tf_op jit(solution)/shard_map/dot_general | solution.py:45
  50.8 0.0 copy-start
  50.8 0.0 copy-start.1
  50.8 0.0 copy-start.2
  50.8 0.0 all-reduce.4.cloned.1.call-update
  50.8 0.0 reduce-scatter.2.cloned.1.call-start
  50.9 0.0 copy-done.3
  50.9 0.0 copy-done.4
  50.9 0.1 select_reduce_fusion
  51.0 103.1 %all-reduce.4.cloned.1.call-done = f32[4096,128]{0,1:T(8,128)} async-done(((f32[4096,128]{0,1:T(8,128)}), f32[4096,128]{0,1:T(8,128)}) %all-reduce.4.cloned.1.call-update) | async-done | bytes 2097168 | tf_op jit(solution)/shard_map/psum | solution.py:50
  154.1 6.1 %convolution_bitcast_fusion.1 = f32[1024,128]{0,1:T(8,128)} fusion(bf16[4096,1024]{1,0:T(8,128)(2,1)} %param.9, f32[4096,128]{0,1:T(8,128)} %all-reduce.4.cloned.1.call-done, f32[4096]{0:T(1024)S(1)} %select_reduce_fusion), kind=kOutput, calls=%fused_computation.2 | convolution fusion | flops 1074790400 | bytes 11026432 | tf_op jit(solution)/shard_map/dot_general | solution.py:52
  160.1 0.0 reduce-scatter.2.cloned.1.call-update
  160.2 21.5 %reduce-scatter.2.cloned.1.call-done = f32[1024,32]{0,1:T(8,128)} async-done(((f32[1024,128]{0,1:T(8,128)}), f32[1024,32]{0,1:T(8,128)}) %reduce-scatter.2.cloned.1.call-update) | async-done | bytes 131088 | tf_op jit(solution)/shard_map/reduce_scatter | solution.py:55
  181.7 1.1 copy.22
  182.8 1.3 collective-permute-start.2
  184.1 4.6 %collective-permute-start.3 = (f32[1,32,32,32]{3,2,1,0:T(8,128)S(1)}, f32[1,32,32,32]{3,2,1,0:T(8,128)S(1)}, u32[]{:S(2)}, u32[]{:S(2)}) collective-permute-start(f32[1,32,32,32]{3,2,1,0:T(8,128)S(1)} %bitcast.12), channel_id=1, source_target_pairs={{0,1},{1,2},{2,3},{3,4},{4,5},{5,6},{6,7},{8,9},{9,10},{10,11},{11... | collective-permute-start | bytes 393224 | tf_op jit(solution)/shard_map/ppermute | solution.py:15
  188.7 9.7 %collective-permute-done.2 = f32[1,32,32,32]{3,2,1,0:T(8,128)S(1)} collective-permute-done((f32[1,32,32,32]{3,2,1,0:T(8,128)S(1)}, f32[1,32,32,32]{3,2,1,0:T(8,128)S(1)}, u32[]{:S(2)}, u32[]{:S(2)}) %collective-permute-start.2) | collective-permute-done | bytes 131104 | tf_op jit(solution)/shard_map/ppermute | solution.py:17
  198.3 11.1 %collective-permute-done.3 = f32[1,32,32,32]{3,2,1,0:T(8,128)S(1)} collective-permute-done((f32[1,32,32,32]{3,2,1,0:T(8,128)S(1)}, f32[1,32,32,32]{3,2,1,0:T(8,128)S(1)}, u32[]{:S(2)}, u32[]{:S(2)}) %collective-permute-start.3) | collective-permute-done | bytes 131104 | tf_op jit(solution)/shard_map/ppermute | solution.py:15
  209.5 0.0 copy-done
  209.5 0.0 copy-done.1
  209.5 0.0 copy-done.2
  209.5 1.2 fusion.12
Async XLA Ops:
  6.5 147.5 %all-reduce.4.cloned.1.call-start = ((), (), s32[]{:S(2)}) async-start(), calls=%async_computation.1 | async-start | bytes 4194304 | tf_op jit(solution)/shard_map/psum | solution.py:50
  6.5 44.3 %copy-start.3 = (s32[4096]{0:T(1024)S(1)}, s32[4096]{0:T(1024)}, u32[]{:S(2)}) copy-start(s32[4096]{0:T(1024)} %param.10) | copy-start | bytes 49156
  6.5 44.3 %copy-start.4 = (f32[8]{0:T(128)S(1)}, f32[8]{0:T(128)}, u32[]{:S(2)}) copy-start(f32[8]{0:T(128)} %param.11) | copy-start | bytes 100
  7.8 16.8 %collective-permute-start = (f32[1,32,32,32]{3,2,1,0:T(8,128)S(1)}, f32[1,32,32,32]{3,2,1,0:T(8,128)S(1)}, u32[]{:S(2)}, u32[]{:S(2)}) collective-permute-start(f32[1,32,32,32]{3,2,1,0:T(8,128)S(1)} %broadcast_multiply_fusion), channel_id=1, source_target_pairs={{1,0},{2,1},{3,2},{4,3},{5,4},{6,5},{7,6},{9,8},{10,9},{11,10},{12... | collective-permute-start | bytes 393224 | tf_op jit(solution)/shard_map/ppermute | solution.py:17
  9.1 26.9 %collective-permute-start.1 = (f32[1,32,32,32]{3,2,1,0:T(8,128)S(1)}, f32[1,32,32,32]{3,2,1,0:T(8,128)S(1)}, u32[]{:S(2)}, u32[]{:S(2)}) collective-permute-start(f32[1,32,32,32]{3,2,1,0:T(8,128)S(1)} %broadcast_multiply_fusion), channel_id=1, source_target_pairs={{0,1},{1,2},{2,3},{3,4},{4,5},{5,6},{6,7},{8,9},{9,10},{10,11},{11... | collective-permute-start | bytes 393224 | tf_op jit(solution)/shard_map/ppermute | solution.py:15
  50.8 158.7 %copy-start = (f32[1,32,32,32]{3,2,1,0:T(8,128)S(1)}, f32[1,32,32,32]{3,2,1,0:T(8,128)}, u32[]{:S(2)}) copy-start(f32[1,32,32,32]{3,2,1,0:T(8,128)} %param.6) | copy-start | bytes 393220
  50.8 158.7 %copy-start.1 = (f32[1,32,32]{2,1,0:T(8,128)S(1)}, f32[1,32,32]{2,1,0:T(8,128)}, u32[]{:S(2)}) copy-start(f32[1,32,32]{2,1,0:T(8,128)} %param.8) | copy-start | bytes 12292
  50.8 158.7 %copy-start.2 = (f32[1,32,32]{2,1,0:T(8,128)S(1)}, f32[1,32,32]{2,1,0:T(8,128)}, u32[]{:S(2)}) copy-start(f32[1,32,32]{2,1,0:T(8,128)} %param.7) | copy-start | bytes 12292
  50.8 130.9 %reduce-scatter.2.cloned.1.call-start = ((), (), s32[]{:S(2)}) async-start(), calls=%async_computation.2 | async-start | bytes 655360 | tf_op jit(solution)/shard_map/reduce_scatter | solution.py:55
  182.8 15.5 %collective-permute-start.2 = (f32[1,32,32,32]{3,2,1,0:T(8,128)S(1)}, f32[1,32,32,32]{3,2,1,0:T(8,128)S(1)}, u32[]{:S(2)}, u32[]{:S(2)}) collective-permute-start(f32[1,32,32,32]{3,2,1,0:T(8,128)S(1)} %bitcast.11), channel_id=1, source_target_pairs={{1,0},{2,1},{3,2},{4,3},{5,4},{6,5},{7,6},{9,8},{10,9},{11,10},{12... | collective-permute-start | bytes 393224 | tf_op jit(solution)/shard_map/ppermute | solution.py:17
  184.1 25.4 %collective-permute-start.3 = (f32[1,32,32,32]{3,2,1,0:T(8,128)S(1)}, f32[1,32,32,32]{3,2,1,0:T(8,128)S(1)}, u32[]{:S(2)}, u32[]{:S(2)}) collective-permute-start(f32[1,32,32,32]{3,2,1,0:T(8,128)S(1)} %bitcast.12), channel_id=1, source_target_pairs={{0,1},{1,2},{2,3},{3,4},{4,5},{5,6},{6,7},{8,9},{9,10},{10,11},{11... | collective-permute-start | bytes 393224 | tf_op jit(solution)/shard_map/ppermute | solution.py:15
Sparse Core Ops, SparseCore 0:
  50.9 103.0 all-reduce.3
  160.3 21.3 reduce-scatter.1
where the time goes:
time: 218 us; the launch traced here: 217 us
  waiting for transfers between devices  167 us (77%)
  matrix products  13.6 us (6%)
  between operations  13.5 us (6%)
  starting transfers between devices  12.7 us (6%)
  blocking collectives  5.79 us (3%)
  other arithmetic  3.88 us (2%)
    psum x1, waiting for transfers between devices, shards(): total = lax.psum(predicted, 'cell')  103 us
    ppermute x2, waiting for transfers between devices, padded_2(): lax.ppermute(tail, axis, [(i, (i + 1) % count) for i in range(ends)])  22.5 us
    reduce_scatter x1, waiting for transfers between devices, shards(): lax.psum_scatter(back, 'dp', scatter_dimension=1, tiled=True)  21.5 us
    ppermute x2, waiting for transfers between devices, padded_2(): lax.ppermute(head, axis, [((i + 1) % count, i) for i in range(ends)])  19.6 us
    ppermute x2, starting transfers between devices, padded_2(): lax.ppermute(tail, axis, [(i, (i + 1) % count) for i in range(ends)])  10.1 us
    dot_general x1, matrix products, shards(): jnp.dot(jacobian, lax.all_gather(prior, 'dp', axis=1, tiled=True), prefer...  7.55 us
    dot_general x1, matrix products, shards(): lax.dot_general(jacobian, weighted, (((0,), (0,)), ((), ())), preferred_e...  6.07 us
    all_gather x1, blocking collectives, shards(): lax.all_gather(prior, 'dp', axis=1, tiled=True)  5.79 us
  transfers between devices with their start and end apart: 6, of which 6 were waited for; matrix products, arithmetic and copies ran while one was open for 0% of the time, Pallas kernels for 0%

commit v1 on v0

v1 whole, which is shorter than its diff:
```python
import functools

import jax
import jax.numpy as jnp
from jax import lax
from jax.experimental import pallas as pl
from jax.experimental.pallas import tpu as pltpu
from jax.sharding import PartitionSpec as P

PIECE = 128
NEAR = 2


def neighbours(field, width):
    cells = field.shape[1]
    lane = lax.broadcasted_iota(jnp.int32, (1, cells), 1)
    column = lane % width
    total = jnp.where(lane >= width, pltpu.roll(field, width, 1), 0.0)
    total += jnp.where(lane < cells - width, pltpu.roll(field, cells - width, 1), 0.0)
    total += jnp.where(column > 0, pltpu.roll(field, 1, 1), 0.0)
    return total + jnp.where(column < width - 1, pltpu.roll(field, cells - 1, 1), 0.0)


def kernel(
    nd, nc, width,
    probes_ref, coef_ref, ids_ref, gw_ref, jac_ref, out_ref,
    jac, halo_out, halo_in, fields, prior, near_out, near_in, keep, far_out, far_in,
    wrow, weighted, acc, back_out, back_in,
    jac_sem, halo_s, halo_r, gat_s, gat_r, near_s, near_r, far_s, far_r, wf_s, wf_r, wn_s, wn_r, dps_s, dps_r, halo2_s, halo2_r,
):
    dp = lax.axis_index("dp")
    cell = lax.axis_index("cell")
    near, far = lax.rem(cell, NEAR), lax.div(cell, NEAR)
    nf = nc // NEAR
    share, cells = probes_ref.shape
    rows = jac.shape[0]
    probes_all = fields.shape[0]
    groups = rows // (PIECE * nc)
    grows = rows // groups
    half = grows // NEAR
    partner = far * NEAR + (1 - near)

    def far_peer(d):
        return lax.rem(far + d, nf) * NEAR + near

    def dp_peer(d):
        return lax.rem(dp + d, nd)

    def jac_copy(g):
        block = pl.ds(g * grows, grows)
        return pltpu.make_async_copy(jac_ref.at[block], jac.at[block], jac_sem.at[g])

    def send(src, dst, ssem, rsem, **device):
        return pltpu.make_async_remote_copy(
            src_ref=src, dst_ref=dst, send_sem=ssem, recv_sem=rsem,
            device_id=device, device_id_type=pl.DeviceIdType.MESH,
        )

    for g in range(groups):
        jac_copy(g).start()

    other = jnp.where(near == 0, cell - 1, cell + 1)
    has_other = jnp.logical_and(other >= 0, other < nc)
    barrier = pltpu.get_barrier_semaphore()

    def greet(**device):
        pl.semaphore_signal(barrier, inc=1, device_id=device, device_id_type=pl.DeviceIdType.MESH)

    greet(cell=partner)

    @pl.when(has_other)
    def _():
        greet(cell=other)

    for d in range(1, nf):
        greet(cell=far_peer(d))
    for d in range(1, nd):
        greet(dp=dp_peer(d))

    coup = coef_ref[1:2, :]
    scaled = coup * probes_ref[...]
    halo_out[0] = scaled.astype(halo_out.dtype)
    pl.semaphore_wait(barrier, 1 + (nf - 1) + (nd - 1) + has_other.astype(jnp.int32))

    def halo(step, up, ssem, rsem):
        slot = 0 if up else 1
        return send(
            halo_out.at[step], halo_in.at[step, slot], ssem.at[slot], rsem.at[slot],
            cell=cell + 1 if up else cell - 1,
        )

    def halo_start(step, ssem, rsem):
        @pl.when(cell < nc - 1)
        def _():
            halo(step, True, ssem, rsem).start()

        @pl.when(cell > 0)
        def _():
            halo(step, False, ssem, rsem).start()

    def halo_sum(step, ssem, rsem):
        @pl.when(cell > 0)
        def _():
            halo(step, True, ssem, rsem).wait_recv()

        @pl.when(cell == 0)
        def _():
            halo_in[step, 0] = jnp.zeros((share, cells), halo_in.dtype)

        @pl.when(cell < nc - 1)
        def _():
            halo(step, False, ssem, rsem).wait_recv()

        @pl.when(cell == nc - 1)
        def _():
            halo_in[step, 1] = jnp.zeros((share, cells), halo_in.dtype)

        return halo_in[step, 0].astype(jnp.float32) + halo_in[step, 1].astype(jnp.float32)

    def halo_end(step, ssem, rsem):
        @pl.when(cell < nc - 1)
        def _():
            halo(step, True, ssem, rsem).wait_send()

        @pl.when(cell > 0)
        def _():
            halo(step, False, ssem, rsem).wait_send()

    halo_start(0, halo_s, halo_r)
    within = neighbours(scaled, width)
    ids = ids_ref[...]
    chosen = jnp.zeros(ids.shape, jnp.float32)
    for j in range(gw_ref.shape[0]):
        chosen = jnp.where(ids == j, gw_ref[j], chosen)
    wrow[...] = chosen

    own = pl.ds(pl.multiple_of(dp * share, share), share)
    total = within + halo_sum(0, halo_s, halo_r)
    fields[own, :] = (coef_ref[0:1, :] * probes_ref[...] - total).astype(fields.dtype)

    def gather(d):
        return send(fields.at[own], fields.at[own], gat_s.at[d], gat_r.at[d], dp=dp_peer(d))

    for d in range(1, nd):
        gather(d).start()
    for d in range(1, nd):
        gather(d).wait_recv()
    prior[...] = fields[...].astype(jnp.float32).T.astype(prior.dtype)

    def near_copy(g):
        return send(near_out.at[g], near_in.at[g], near_s.at[g], near_r.at[g], cell=partner)

    def far_copy(g, d):
        piece = pl.ds(pl.multiple_of(lax.rem(far + d, nf) * PIECE, PIECE), PIECE)
        return send(
            far_out.at[g, piece], far_in.at[g, d], far_s.at[g, d], far_r.at[g, d], cell=far_peer(d)
        )

    def wf_copy(g, d):
        k = (g * NEAR + near) * nf + far
        return send(weighted.at[k], weighted.at[k], wf_s.at[g, d], wf_r.at[g, d], cell=far_peer(d))

    def wn_copy(g):
        block = pl.ds((g * NEAR + near) * nf, nf)
        return send(weighted.at[block], weighted.at[block], wn_s.at[g], wn_r.at[g], cell=partner)

    def product(start, count):
        return jnp.dot(
            jac[pl.ds(pl.multiple_of(start, count), count), :], prior[...],
            preferred_element_type=jnp.float32,
        )

    def step_near(g):
        jac_copy(g).wait()
        near_out[g] = product(g * grows + (1 - near) * half, half).astype(near_out.dtype)
        near_copy(g).start()
        keep[g] = product(g * grows + near * half, half)

    def step_far(g):
        near_copy(g).wait_recv()
        summed = keep[g] + near_in[g].astype(jnp.float32)
        keep[g] = summed
        far_out[g] = summed.astype(far_out.dtype)
        for d in range(1, nf):
            far_copy(g, d).start()

    def step_weigh(g):
        total = keep[g, pl.ds(pl.multiple_of(far * PIECE, PIECE), PIECE), :]
        for d in range(1, nf):
            far_copy(g, d).wait_recv()
            total = total + far_in[g, d].astype(jnp.float32)
        k = (g * NEAR + near) * nf + far
        weighted[k] = (total.T * wrow[pl.ds(k, 1), :]).astype(weighted.dtype)
        for d in range(1, nf):
            wf_copy(g, d).start()

    def step_back(g):
        for d in range(1, nf):
            wf_copy(g, d).wait_recv()
        wn_copy(g).start()

    def step_product(g):
        wn_copy(g).wait_recv()
        pieces = grows // PIECE
        lhs = jnp.concatenate([weighted[g * pieces + k] for k in range(pieces)], axis=1)
        part = jnp.dot(lhs, jac[g * grows:(g + 1) * grows, :], preferred_element_type=jnp.float32)
        acc[...] = part if g == 0 else acc[...] + part

    steps = (step_near, step_far, step_weigh, step_back, step_product)
    for tick in range(groups + len(steps) - 1):
        for lag, step in enumerate(steps):
            if 0 <= tick - lag < groups:
                step(tick - lag)

    def scatter(d):
        return send(back_out.at[d], back_in.at[d], dps_s.at[d], dps_r.at[d], dp=dp_peer(d))

    for d in range(1, nd):
        block = pl.ds(pl.multiple_of(dp_peer(d) * share, share), share)
        back_out[d] = acc[block, :].astype(back_out.dtype)
        scatter(d).start()
    mine = acc[own, :]
    for d in range(1, nd):
        scatter(d).wait_recv()
        mine = mine + back_in[d].astype(jnp.float32)
    halo_out[1] = mine.astype(halo_out.dtype)
    halo_start(1, halo2_s, halo2_r)
    within = neighbours(mine, width)
    start = probes_ref[...] + coef_ref[0:1, :] * mine
    out_ref[...] = start - coup * (within + halo_sum(1, halo2_s, halo2_r))

    halo_end(0, halo_s, halo_r)
    halo_end(1, halo2_s, halo2_r)
    for d in range(1, nd):
        gather(d).wait_send()
        scatter(d).wait_send()
    for g in range(groups):
        near_copy(g).wait_send()
        wn_copy(g).wait_send()
        for d in range(1, nf):
            far_copy(g, d).wait_send()
            wf_copy(g, d).wait_send()


def shards(nd, nc, probes, diag_coef, coupling, jacobian, group_ids, group_weights):
    depth, height, width, share = probes.shape
    cells = depth * height * width
    rows = jacobian.shape[0]
    nf = nc // NEAR
    groups = rows // (PIECE * nc)
    grows = rows // groups
    half = grows // NEAR
    everyone = share * nd
    assert depth == 1 and nc % NEAR == 0 and groups * PIECE * nc == rows

    flat = probes.reshape(cells, share).T
    coefs = jnp.concatenate([diag_coef.reshape(1, cells), coupling.reshape(1, cells)], axis=0)
    low, dma = jnp.bfloat16, pltpu.SemaphoreType.DMA
    vmem = pl.BlockSpec(memory_space=pltpu.VMEM)
    out = pl.pallas_call(
        functools.partial(kernel, nd, nc, width),
        out_shape=jax.ShapeDtypeStruct((share, cells), jnp.float32),
        in_specs=[
            vmem, vmem, vmem,
            pl.BlockSpec(memory_space=pltpu.SMEM),
            pl.BlockSpec(memory_space=pl.ANY),
        ],
        out_specs=vmem,
        scratch_shapes=[
            pltpu.VMEM((rows, cells), low),
            pltpu.VMEM((2, share, cells), low),
            pltpu.VMEM((2, 2, share, cells), low),
            pltpu.VMEM((everyone, cells), low),
            pltpu.VMEM((cells, everyone), low),
            pltpu.VMEM((groups, half, everyone), low),
            pltpu.VMEM((groups, half, everyone), low),
            pltpu.VMEM((groups, half, everyone), jnp.float32),
            pltpu.VMEM((groups, half, everyone), low),
            pltpu.VMEM((groups, nf, PIECE, everyone), low),
            pltpu.VMEM((rows // PIECE, PIECE), jnp.float32),
            pltpu.VMEM((rows // PIECE, everyone, PIECE), low),
            pltpu.VMEM((everyone, cells), jnp.float32),
            pltpu.VMEM((nd, share, cells), low),
            pltpu.VMEM((nd, share, cells), low),
            dma((groups,)),
            dma((2,)), dma((2,)),
            dma((nd,)), dma((nd,)),
            dma((groups,)), dma((groups,)),
            dma((groups, nf)), dma((groups, nf)),
            dma((groups, nf)), dma((groups, nf)),
            dma((groups,)), dma((groups,)),
            dma((nd,)), dma((nd,)),
            dma((2,)), dma((2,)),
        ],
        compiler_params=pltpu.CompilerParams(
            collective_id=0, has_side_effects=True, vmem_limit_bytes=56 * 1024 * 1024
        ),
        cost_estimate=pl.CostEstimate(
            flops=4 * rows * cells * everyone, bytes_accessed=2 * rows * cells, transcendentals=0
        ),
    )(flat, coefs, group_ids.reshape(rows // PIECE, PIECE), group_weights, jacobian)
    return out.T.reshape(depth, height, width, share)


def solution(mesh):
    return jax.shard_map(
        functools.partial(shards, mesh.shape["dp"], mesh.shape["cell"]),
        mesh=mesh,
        in_specs=(
            P("cell", None, None, "dp"),
            P("cell", None, None),
            P("cell", None, None),
            P("dp", "cell"),
            P("dp"),
            P(),
        ),
        out_specs=P("cell", None, None, "dp"),
        check_vma=False,
    )
```

time: 218 us -> 64.5 us (0.30)
  waiting for transfers between devices: 167 us -> 0 us
  Pallas kernels: 0 us -> 57.8 us
  matrix products: 13.6 us -> 0 us
  between operations: 13.5 us -> 0.01 us
  starting transfers between devices: 12.7 us -> 0 us
  blocking collectives: 5.79 us -> 0 us
  local copies, waits for them, and re-layouts: 1.23 us -> 5.37 us
  other arithmetic: 3.88 us -> 0.61 us
    psum x1 -> x0, waiting for transfers between devices: 103 us -> none  [shards(): total = lax.psum(predicted, 'cell')]
    pallas_call x0 -> x1, Pallas kernels: none -> 57.8 us  [shards(): pl.pallas_call(functools.partial(kernel, nd, nc, width), out_shape=jax.Sh...]
    ppermute x4 -> x0, waiting for transfers between devices: 42.1 us -> none  [the longest x2 22.5 us: padded_2(): lax.ppermute(tail, axis, [(i, (i + 1) % count) for i in range(ends)])]
    reduce_scatter x1 -> x0, waiting for transfers between devices: 21.5 us -> none  [shards(): lax.psum_scatter(back, 'dp', scatter_dimension=1, tiled=True)]
    dot_general x2 -> x0, matrix products: 13.6 us -> none  [the longest x1 7.55 us: shards(): jnp.dot(jacobian, lax.all_gather(prior, 'dp', axis=1, tiled=True), prefer...]
    ppermute x4 -> x0, starting transfers between devices: 12.7 us -> none  [the longest x2 10.1 us: padded_2(): lax.ppermute(tail, axis, [(i, (i + 1) % count) for i in range(ends)])]
    all_gather x1 -> x0, blocking collectives: 5.79 us -> none  [shards(): lax.all_gather(prior, 'dp', axis=1, tiled=True)]
    reshape x2 -> x4, local copies, waits for them, and re-layouts: 1.21 us -> 5.37 us  [the longest x1 1.9 us: shards(): return out.T.reshape(depth, height, width, share)]
  transfers between devices with their start and end apart: 6 -> 0, of which waited for: 6 -> 0; matrix products, arithmetic and copies ran while one was open for 0% -> 0% of each run, Pallas kernels for 0% -> 0%
where the time goes in v1:
time: 64.5 us; the launch traced here: 63.8 us
  Pallas kernels  57.8 us (90%)
  local copies, waits for them, and re-layouts  5.37 us (8%)
    pallas_call x1, Pallas kernels, shards(): pl.pallas_call(functools.partial(kernel, nd, nc, width), out_shape=jax.Sh...  57.8 us
    reshape x1, local copies, waits for them, and re-layouts, shards(): return out.T.reshape(depth, height, width, share)  1.9 us
    reshape x1, local copies, waits for them, and re-layouts, shards(): flat = probes.reshape(cells, share).T  1.87 us

profile of v1, /device:TPU:0, one launch (start us, length us, event | category | flops | bytes accessed | tf_op | source)
XLA Modules:
  0.0 63.8 jit_solution(4466029951360136557)
XLA Ops:
  0.0 0.8 %reshape.16 = f32[1,1024]{1,0:T(1,128)S(1)} reshape(f32[1,32,32]{2,1,0:T(8,128)} %param.7) | data formatting | bytes 8192 | tf_op jit(solution)/shard_map/reshape | solution.py:257
  0.8 0.8 %reshape.17 = f32[1,1024]{1,0:T(1,128)S(1)} reshape(f32[1,32,32]{2,1,0:T(8,128)} %param.8) | data formatting | bytes 8192 | tf_op jit(solution)/shard_map/reshape | solution.py:257
  1.6 0.6 pad_maximum_fusion.coef_ref
  2.2 1.9 %copy.9 = f32[1024,32]{0,1:T(8,128)} copy(f32[1024,32]{1,0:T(8,128)} %bitcast.7) | data formatting | bytes 262144 | tf_op jit(solution)/shard_map/reshape | solution.py:256
  4.1 57.8 %shard_map.64 = f32[32,1024]{1,0:T(8,128)} custom-call(f32[32,1024]{1,0:T(8,128)} %bitcast.6, f32[2,1024]{1,0:T(2,128)} %pad_maximum_fusion.coef_ref, s32[32,128]{1,0:T(8,128)} %bitcast.8, f32[8]{0:T(128)} %gw_ref.1, bf16[4096,1024]{1,0:T(8,128)(2,1)} %jac_ref.1), custom_call_target="tpu_custom_call" | custom-call | flops 2147483648 | bytes 8388608 | tf_op jit(solution)/shard_map/pallas_call | solution.py:260
  61.9 1.9 %copy.10 = f32[1024,32]{1,0:T(8,128)} copy(f32[1024,32]{0,1:T(8,128)} %bitcast.5) | data formatting | bytes 262144 | tf_op jit(solution)/shard_map/reshape | solution.py:302

commit v2 on v1

v2 whole, which is shorter than its diff:
```python
import functools

import jax
import jax.numpy as jnp
from jax import lax
from jax.experimental import pallas as pl
from jax.experimental.pallas import tpu as pltpu
from jax.sharding import PartitionSpec as P

PIECE = 128
PARTS = 2


def as_row(ref, cells):
    height, width = ref.shape
    lane = lax.broadcasted_iota(jnp.int32, (width, cells), 1)
    spread = (lane % width == lax.broadcasted_iota(jnp.int32, (width, cells), 0)).astype(jnp.float32)
    wide = jnp.dot(
        ref[...], spread, precision=lax.Precision.HIGHEST, preferred_element_type=jnp.float32
    )
    lane = lax.broadcasted_iota(jnp.int32, (height, cells), 1)
    mine = lane // width == lax.broadcasted_iota(jnp.int32, (height, cells), 0)
    return jnp.sum(jnp.where(mine, wide, 0.0), axis=0, keepdims=True)


def neighbours(field, width):
    cells = field.shape[1]
    lane = lax.broadcasted_iota(jnp.int32, (1, cells), 1)
    column = lane % width
    total = jnp.where(lane >= width, pltpu.roll(field, width, 1), 0.0)
    total += jnp.where(lane < cells - width, pltpu.roll(field, cells - width, 1), 0.0)
    total += jnp.where(column > 0, pltpu.roll(field, 1, 1), 0.0)
    return total + jnp.where(column < width - 1, pltpu.roll(field, cells - 1, 1), 0.0)


def kernel(
    nd, nc,
    probes_ref, diag_ref, coup_ref, ids_ref, gw_ref, jac_ref, out_ref,
    jac, flat, halo_out, halo_in, fields, prior, near_out, near_in, keep, far_out, far_in,
    wrow, weighted, acc, back_out, back_in, own_sum,
    jac_sem, halo_s, halo_r, gat_s, gat_r, sum_s, sum_r, put_s, put_r, dps_s, dps_r,
):
    dp = lax.axis_index("dp")
    cell = lax.axis_index("cell")
    cells, share = probes_ref.shape
    width = diag_ref.shape[1]
    rows = jac.shape[0]
    groups = rows // (PIECE * nc)
    grows = rows // groups
    half = grows // 2
    levels = nc.bit_length() - 1
    part = cells // PARTS

    def bit(b):
        return lax.rem(lax.div(cell, 1 << b), 2)

    def peer(b):
        return cell + (1 - 2 * bit(b)) * (1 << b)

    def order(g):
        return (1, 0, *range(2, levels)) if g == 1 else tuple(range(levels))

    def dp_peer(d):
        return lax.rem(dp + d, nd)

    def jac_copy(g):
        block = pl.ds(g * grows, grows)
        return pltpu.make_async_copy(jac_ref.at[block], jac.at[block], jac_sem.at[g])

    def send(src, dst, ssem, rsem, **device):
        return pltpu.make_async_remote_copy(
            src_ref=src, dst_ref=dst, send_sem=ssem, recv_sem=rsem,
            device_id=device, device_id_type=pl.DeviceIdType.MESH,
        )

    other = cell + 2 * bit(0) - 1
    has_other = jnp.logical_and(other >= 0, other < nc)
    barrier = pltpu.get_barrier_semaphore()

    def greet(**device):
        pl.semaphore_signal(barrier, inc=1, device_id=device, device_id_type=pl.DeviceIdType.MESH)

    @pl.when(has_other)
    def _():
        greet(cell=other)

    for b in range(levels):
        greet(cell=peer(b))
    for d in range(1, nd):
        greet(dp=dp_peer(d))
    for g in range(groups):
        jac_copy(g).start()

    coup = as_row(coup_ref, cells)
    flat[...] = probes_ref[...].T
    scaled = coup * flat[...]

    def columns(h):
        return pl.ds(h * part, part)

    for h in range(PARTS):
        halo_out[0, h] = scaled[:, h * part:(h + 1) * part].astype(halo_out.dtype)
    pl.semaphore_wait(barrier, levels + (nd - 1) + has_other.astype(jnp.int32))

    def halo(step, h, up):
        slot = 0 if up else 1
        return send(
            halo_out.at[step, h], halo_in.at[step, h, slot],
            halo_s.at[step, h, slot], halo_r.at[step, h, slot],
            cell=cell + 1 if up else cell - 1,
        )

    def halo_start(step, h):
        @pl.when(cell < nc - 1)
        def _():
            halo(step, h, True).start()

        @pl.when(cell > 0)
        def _():
            halo(step, h, False).start()

    def halo_sum(step, h):
        @pl.when(cell > 0)
        def _():
            halo(step, h, True).wait_recv()

        @pl.when(cell == 0)
        def _():
            halo_in[step, h, 0] = jnp.zeros((share, part), halo_in.dtype)

        @pl.when(cell < nc - 1)
        def _():
            halo(step, h, False).wait_recv()

        @pl.when(cell == nc - 1)
        def _():
            halo_in[step, h, 1] = jnp.zeros((share, part), halo_in.dtype)

        return halo_in[step, h, 0].astype(jnp.float32) + halo_in[step, h, 1].astype(jnp.float32)

    def halo_end(step, h):
        @pl.when(cell < nc - 1)
        def _():
            halo(step, h, True).wait_send()

        @pl.when(cell > 0)
        def _():
            halo(step, h, False).wait_send()

    for h in range(PARTS):
        halo_start(0, h)
    diag = as_row(diag_ref, cells)
    within = diag * flat[...] - neighbours(scaled, width)
    ids = ids_ref[...]
    chosen = jnp.zeros(ids.shape, jnp.float32)
    for j in range(gw_ref.shape[0]):
        chosen = jnp.where(ids == j, gw_ref[j], chosen)
    wrow[...] = chosen

    own = pl.ds(pl.multiple_of(dp * share, share), share)

    def gather(d, h):
        block = fields.at[h, own]
        return send(block, block, gat_s.at[d, h], gat_r.at[d, h], dp=dp_peer(d))

    for h in range(PARTS):
        total = within[:, h * part:(h + 1) * part] - halo_sum(0, h)
        fields[h, own] = total.astype(fields.dtype)
        for d in range(1, nd):
            gather(d, h).start()
    for h in range(PARTS):
        for d in range(1, nd):
            gather(d, h).wait_recv()
        prior[columns(h), :] = fields[h].astype(jnp.float32).T.astype(prior.dtype)

    def block(g, i):
        start = 0
        for level in range(1, i + 1):
            size = half >> level
            mine = bit(order(g)[level])
            kept, sent, start = start + mine * size, start + (1 - mine) * size, start + mine * size
        return kept, sent, size

    def ds(start, size):
        return pl.ds(pl.multiple_of(start, size), size)

    def sum_copy(g, i):
        ssem, rsem, to = sum_s.at[g, i], sum_r.at[g, i], peer(order(g)[i])
        if i == 0:
            return send(near_out.at[g], near_in.at[g], ssem, rsem, cell=to)
        kept, sent, size = block(g, i)
        return send(far_out.at[g, ds(sent, size)], far_in.at[g, ds(kept, size)], ssem, rsem, cell=to)

    def arrived(g, i, skip, size):
        if i == 0:
            return near_in[g, ds(skip, size), :].astype(jnp.float32)
        return far_in[g, ds(block(g, i)[1] + skip, size), :].astype(jnp.float32)

    def place(g):
        where = 0
        for b in order(g):
            where = where * 2 + bit(b)
        return where

    def put_copy(g, i):
        count = 1 << (levels - 1 - i)
        pieces = weighted.at[pl.ds(g * nc + lax.div(place(g), count) * count, count)]
        return send(pieces, pieces, put_s.at[g, i], put_r.at[g, i], cell=peer(order(g)[i]))

    def product(start, count):
        return jnp.dot(
            jac[pl.ds(pl.multiple_of(start, count), count), :], prior[...],
            preferred_element_type=jnp.float32,
        )

    def first(g):
        mine = bit(order(g)[0])
        jac_copy(g).wait()
        near_out[g] = product(g * grows + (1 - mine) * half, half).astype(near_out.dtype)
        sum_copy(g, 0).start()
        keep[g] = product(g * grows + mine * half, half)

    def add(g, i):
        sum_copy(g, i - 1).wait_recv()
        kept, sent, size = block(g, i)
        mine = bit(order(g)[i])
        leaves = keep[g, ds(sent, size), :] + arrived(g, i - 1, (1 - mine) * size, size)
        far_out[g, ds(sent, size), :] = leaves.astype(far_out.dtype)
        sum_copy(g, i).start()
        keep[g, ds(kept, size), :] += arrived(g, i - 1, mine * size, size)

    def weigh(g):
        sum_copy(g, levels - 1).wait_recv()
        kept, _, size = block(g, levels - 1)
        total = keep[g, ds(kept, size), :] + arrived(g, levels - 1, 0, size)
        k = g * nc + place(g)
        weighted[k] = (total.T * wrow[pl.ds(k, 1), :]).astype(weighted.dtype)
        put_copy(g, levels - 1).start()

    def hand(g, i):
        put_copy(g, i + 1).wait_recv()
        put_copy(g, i).start()

    def scatter(d, h):
        return send(
            back_out.at[d, h], back_in.at[d, h], dps_s.at[d, h], dps_r.at[d, h], dp=dp_peer(d)
        )

    def last(g):
        put_copy(g, 0).wait_recv()
        lhs = jnp.concatenate([weighted[g * nc + k] for k in range(nc)], axis=1)
        for h in range(PARTS):
            back = jnp.dot(
                lhs, jac[pl.ds(g * grows, grows), columns(h)], preferred_element_type=jnp.float32
            )
            acc[h] = back if g == 0 else acc[h] + back
            if g == groups - 1:
                for d in range(1, nd):
                    theirs = pl.ds(pl.multiple_of(dp_peer(d) * share, share), share)
                    back_out[d, h] = acc[h, theirs].astype(back_out.dtype)
                    scatter(d, h).start()

    steps = [first]
    steps += [functools.partial(add, i=i) for i in range(1, levels)]
    steps += [weigh]
    steps += [functools.partial(hand, i=i) for i in reversed(range(levels - 1))]
    steps += [last]
    for tick in range(groups + len(steps) - 1):
        for lag, step in enumerate(steps):
            if 0 <= tick - lag < groups:
                step(tick - lag)

    for h in range(PARTS):
        mine = acc[h, own]
        for d in range(1, nd):
            scatter(d, h).wait_recv()
            mine = mine + back_in[d, h].astype(jnp.float32)
        own_sum[:, columns(h)] = mine
        halo_out[1, h] = mine.astype(halo_out.dtype)
        halo_start(1, h)
    mine = own_sum[...]
    within = neighbours(mine, width)
    start = flat[...] + diag * mine - coup * within
    for h in range(PARTS):
        cut = slice(h * part, (h + 1) * part)
        out_ref[columns(h), :] = (start[:, cut] - coup[:, cut] * halo_sum(1, h)).T

    for h in range(PARTS):
        halo_end(0, h)
        halo_end(1, h)
        for d in range(1, nd):
            gather(d, h).wait_send()
            scatter(d, h).wait_send()
    for g in range(groups):
        for i in range(levels):
            sum_copy(g, i).wait_send()
            put_copy(g, i).wait_send()


def shards(nd, nc, probes, diag_coef, coupling, jacobian, group_ids, group_weights):
    depth, height, width, share = probes.shape
    cells = depth * height * width
    rows = jacobian.shape[0]
    levels = nc.bit_length() - 1
    groups = rows // (PIECE * nc)
    half = rows // groups // 2
    everyone = share * nd
    part = cells // PARTS
    assert depth == 1 and nc == 1 << levels and levels >= 2 and groups * PIECE * nc == rows

    low, dma = jnp.bfloat16, pltpu.SemaphoreType.DMA
    vmem = pl.BlockSpec(memory_space=pltpu.VMEM)
    out = pl.pallas_call(
        functools.partial(kernel, nd, nc),
        out_shape=jax.ShapeDtypeStruct((cells, share), jnp.float32),
        in_specs=[
            vmem, vmem, vmem, vmem,
            pl.BlockSpec(memory_space=pltpu.SMEM),
            pl.BlockSpec(memory_space=pl.ANY),
        ],
        out_specs=vmem,
        scratch_shapes=[
            pltpu.VMEM((rows, cells), low),
            pltpu.VMEM((share, cells), jnp.float32),
            pltpu.VMEM((2, PARTS, share, part), low),
            pltpu.VMEM((2, PARTS, 2, share, part), low),
            pltpu.VMEM((PARTS, everyone, part), low),
            pltpu.VMEM((cells, everyone), low),
            pltpu.VMEM((groups, half, everyone), low),
            pltpu.VMEM((groups, half, everyone), low),
            pltpu.VMEM((groups, half, everyone), jnp.float32),
            pltpu.VMEM((groups, half, everyone), low),
            pltpu.VMEM((groups, half, everyone), low),
            pltpu.VMEM((rows // PIECE, PIECE), jnp.float32),
            pltpu.VMEM((rows // PIECE, everyone, PIECE), low),
            pltpu.VMEM((PARTS, everyone, part), jnp.float32),
            pltpu.VMEM((nd, PARTS, share, part), low),
            pltpu.VMEM((nd, PARTS, share, part), low),
            pltpu.VMEM((share, cells), jnp.float32),
            dma((groups,)),
            dma((2, PARTS, 2)), dma((2, PARTS, 2)),
            dma((nd, PARTS)), dma((nd, PARTS)),
            dma((groups, levels)), dma((groups, levels)),
            dma((groups, levels)), dma((groups, levels)),
            dma((nd, PARTS)), dma((nd, PARTS)),
        ],
        compiler_params=pltpu.CompilerParams(
            collective_id=0, has_side_effects=True, vmem_limit_bytes=56 * 1024 * 1024
        ),
        cost_estimate=pl.CostEstimate(
            flops=4 * rows * cells * everyone, bytes_accessed=2 * rows * cells, transcendentals=0
        ),
    )(
        probes.reshape(cells, share),
        diag_coef.reshape(height, width),
        coupling.reshape(height, width),
        group_ids.reshape(rows // PIECE, PIECE),
        group_weights,
        jacobian,
    )
    return out.reshape(depth, height, width, share)


def solution(mesh):
    return jax.shard_map(
        functools.partial(shards, mesh.shape["dp"], mesh.shape["cell"]),
        mesh=mesh,
        in_specs=(
            P("cell", None, None, "dp"),
            P("cell", None, None),
            P("cell", None, None),
            P("dp", "cell"),
            P("dp"),
            P(),
        ),
        out_specs=P("cell", None, None, "dp"),
        check_vma=False,
    )
```

time: 64.5 us -> 59.3 us (0.919)
  local copies, waits for them, and re-layouts: 5.37 us -> 1.87 us
    reshape x4 -> x0, local copies, waits for them, and re-layouts: 5.37 us -> none  [the longest x1 1.9 us: shards(): return out.T.reshape(depth, height, width, share)]
    unnamed x0 -> x1, local copies, waits for them, and re-layouts: none -> 1.87 us
where the time goes in v2:
time: 59.3 us; the launch traced here: 59.1 us
  Pallas kernels  57.2 us (96%)
  local copies, waits for them, and re-layouts  1.87 us (3%)
    pallas_call x1, Pallas kernels, shards(): pl.pallas_call(functools.partial(kernel, nd, nc), out_shape=jax.ShapeDtyp...  57.2 us
    unnamed x1, local copies, waits for them, and re-layouts  1.87 us

profile of v2, /device:TPU:0, one launch (start us, length us, event | category | flops | bytes accessed | tf_op | source)
XLA Modules:
  0.0 59.1 jit_solution(1843101532988079835)
XLA Ops:
  0.0 57.2 %shard_map.64 = f32[1024,32]{1,0:T(8,128)} custom-call(f32[1024,32]{1,0:T(8,128)} %bitcast.6, f32[32,32]{1,0:T(8,128)} %bitcast.7, f32[32,32]{1,0:T(8,128)} %bitcast.8, s32[32,128]{1,0:T(8,128)} %bitcast.9, f32[8]{0:T(128)} %gw_ref.1, bf16[4096,1024]{1,0:T(8,128)(2,1)} %jac_ref.1), custom_call_target="tpu_custom_call" | custom-call | flops 2147483648 | bytes 8388608 | tf_op jit(solution)/shard_map/pallas_call | solution.py:313
  57.2 1.9 %copy.8 = f32[1,32,32,32]{3,2,1,0:T(8,128)} copy(f32[1,32,32,32]{3,2,1,0:T(8,128)} %bitcast.5) | data formatting | bytes 262144
